TPU v7x, 32 devices: a whole 2x2x4 slice. The times are simulated.
32 devices in a mesh: leaf: 32 (over z, y, x, core).
Axes of the slice: x: 2, y: 2, z: 4, core: 2. Of those that a mesh axis runs over, the one named last changes fastest.
Arguments:
- points: bfloat16 [64, 131072], P(None, 'leaf'), may hold values from -3 to 7
- weights: bfloat16 [32, 131072], P(None, 'leaf'), may hold values from -6 to 6
- skel_index: int32 [16384], P('leaf'), may hold values from 0 to 4095, as said below
- assign: int32 [131072], P('leaf'), may hold values from 0 to 511
- near_leaf: int32 [256, 12], replicated, may hold values from 0 to 255, as said below
- near_count: int32 [256], replicated, may hold values from 6 to 12
Outputs:
- near_field: float32 [32, 131072], P(None, 'leaf')
- far_field: float32 [32, 131072], P(None, 'leaf')
Inputs may be any that keep to these rules, and one draw needn't show every extreme that they name: `skel_index`: each device's 512 entries are distinct. `near_leaf`: leaf id g belongs to device g // 8. For each device r, its 96 entries read leaf by leaf and taken in runs of 32 - 1 (the last run may be shorter) name leaves of devices other than r, of distinct devices within a run; so a device reads at most 4 blocks from any one device, and this is reached.
All inputs are finite; a program needn't handle non-finite values.
Results may differ from a plain program's by a relative error of at most 0.0088.
Values may be sent and summed in bfloat16 or wider, within the bound.
A program may use at most 128 MiB of HBM per device.

v0:
```python
import math

import jax
import jax.numpy as jnp
from jax import lax
from jax.sharding import PartitionSpec as P

D = 64
LEAF = 512
SKEL = 512
NEAR = 12


def from_partner(block, axis, apart):
    count = lax.axis_size(axis)
    route = []
    for low in range(count):
        high = low | 1 << apart
        if high != low and high < count:
            route += [(low, high), (high, low)]
    return lax.ppermute(block, axis, route)


def kernel_apply(targets, sources, source_w):
    inner_prod = lax.dot_general(
        sources, targets, (((0,), (0,)), ((), ())), preferred_element_type=jnp.float32
    )
    target_sq = jnp.sum(jnp.square(targets.astype(jnp.float32)), axis=0)
    source_sq = jnp.sum(jnp.square(sources.astype(jnp.float32)), axis=0)
    sq_dist = source_sq[:, None] + target_sq[None, :] - 2.0 * inner_prod
    kernel_tile = jnp.exp(sq_dist * (-1.0 / D)).astype(jnp.bfloat16)
    return jnp.dot(source_w, kernel_tile, preferred_element_type=jnp.float32)


def fold_child(node_stack):
    half_width = node_stack.shape[-1] // 2
    node_weights = node_stack[..., D:, :half_width].astype(jnp.float32) + node_stack[
        ..., D:, half_width:
    ].astype(jnp.float32)
    return jnp.concatenate(
        [node_stack[..., :D, :half_width], node_weights.astype(jnp.bfloat16)], axis=-2
    )


def merge_pair(lower_child, upper_child):
    return jnp.concatenate([fold_child(lower_child), fold_child(upper_child)], axis=-1)


def self_term(leaf_block):
    return kernel_apply(leaf_block[:D], leaf_block[:D], leaf_block[D:])


def per_device(points, weights, skel_index, assign, near_leaf, near_count):
    n_dev = lax.axis_size("leaf")
    my_index = lax.axis_index("leaf")
    depth_count = n_dev.bit_length() - 1
    rhs_width = weights.shape[0]
    p_dev = points.shape[1]
    leaves_dev = p_dev // LEAF
    member = (assign[None, :] == jnp.arange(SKEL, dtype=jnp.int32)[:, None]).astype(jnp.bfloat16)
    base_weights = lax.dot_general(
        weights, member, (((1,), (1,)), ((), ())), preferred_element_type=jnp.float32
    )
    base_node = jnp.concatenate([points[:, skel_index], base_weights.astype(jnp.bfloat16)], axis=0)
    far_sum = jnp.zeros((rhs_width, p_dev), jnp.float32)
    current = base_node
    for depth_bit in range(depth_count):
        partner = from_partner(current, "leaf", depth_bit)
        far_sum = far_sum + kernel_apply(points, partner[:D], partner[D:])
        if depth_bit + 1 < depth_count:
            upper_bit = my_index >> depth_bit & 1
            lower_child = jnp.where(upper_bit == 0, current, partner)
            upper_child = jnp.where(upper_bit == 0, partner, current)
            current = merge_pair(lower_child, upper_child)
    far_field = far_sum * (4.0 / math.sqrt(p_dev * n_dev))
    leaf_blocks = (
        jnp.concatenate([points, weights], axis=0)
        .reshape(D + rhs_width, leaves_dev, LEAF)
        .transpose(1, 0, 2)
    )
    slot_count = leaves_dev * NEAR
    capacity = (slot_count + n_dev - 2) // (n_dev - 1)
    owner_dev = (near_leaf // leaves_dev).reshape(n_dev, slot_count)
    owner_leaf = (near_leaf % leaves_dev).reshape(n_dev, slot_count)
    slot_round = jnp.arange(slot_count, dtype=jnp.int32) // (n_dev - 1)
    rounds = jnp.arange(capacity, dtype=jnp.int32)
    asked_here = (owner_dev == my_index)[:, None, :] & (
        slot_round[None, None, :] == rounds[None, :, None]
    )
    picked = jnp.sum(jnp.where(asked_here, owner_leaf[:, None, :], 0), axis=-1)
    my_owner = lax.dynamic_index_in_dim(owner_dev, my_index, 0, keepdims=False)
    own_terms = jax.vmap(self_term)(leaf_blocks)
    outgoing = leaf_blocks[picked]
    incoming = lax.all_to_all(outgoing, "leaf", split_axis=0, concat_axis=0, tiled=True)
    arrived = incoming[my_owner.reshape(leaves_dev, NEAR), slot_round.reshape(leaves_dev, NEAR)]
    my_count = lax.dynamic_slice_in_dim(near_count, my_index * leaves_dev, leaves_dev)
    per_leaf = []
    for leaf_pos in range(leaves_dev):
        target = leaf_blocks[leaf_pos, :D]
        leaf_arrived = arrived[leaf_pos]

        def add_slot(slot_step, running):
            source_block = lax.dynamic_index_in_dim(leaf_arrived, slot_step, 0, keepdims=False)
            return running + kernel_apply(target, source_block[:D], source_block[D:])

        per_leaf.append(lax.fori_loop(0, my_count[leaf_pos], add_slot, own_terms[leaf_pos]))
    near_sum = jnp.stack(per_leaf)
    near_field = near_sum.transpose(1, 0, 2).reshape(rhs_width, p_dev) * (
        4.0 / math.sqrt(LEAF * (NEAR + 1))
    )
    return (near_field, far_field)


def solution(mesh):
    return jax.shard_map(
        per_device,
        mesh=mesh,
        in_specs=(P(None, "leaf"), P(None, "leaf"), P("leaf"), P("leaf"), P(), P()),
        out_specs=(P(None, "leaf"), P(None, "leaf")),
        check_vma=False,
    )
```

profile of v0, /device:TPU:0, one launch (start us, length us, event | category | flops | bytes accessed | tf_op | source)
XLA Modules:
  0.0 588.6 jit_solution(8537867928424306284)
XLA Ops:
  4.2 8.2 %gather_fusion = bf16[128,96,512]{2,1,0:T(8,128)(2,1)} fusion(bf16[8,96,512]{2,1,0:T(8,128)(2,1)S(1)} %bitcast.211, s32[1024]{0:T(1024)S(1)} %get-tuple-element.373), kind=kCustom, calls=%fused_computation | custom fusion | bytes 25166336 | tf_op jit(solution)/shard_map/gather | solution.py:93
  12.4 7.5 %all-to-all-start = ((bf16[32,4,96,512]{3,2,1,0:T(8,128)(2,1)}), bf16[32,4,96,512]{3,2,1,0:T(8,128)(2,1)}, u32[]{:S(2)}, u32[]{:S(2)}) async-start(bf16[32,4,96,512]{3,2,1,0:T(8,128)(2,1)} %bitcast.215), calls=%async_computation | async-start | bytes 25165824 | tf_op jit(solution)/shard_map/all_to_all | solution.py:94
  24.5 3.0 fusion.126
  31.4 79.1 %collective-permute-done.1 = bf16[96,512]{0,1:T(8,128)(2,1)S(1)} collective-permute-done((bf16[96,512]{0,1:T(8,128)(2,1)S(1)}, bf16[96,512]{0,1:T(8,128)(2,1)S(1)}, u32[]{:S(2)}, u32[]{:S(2)}) %collective-permute-start.1) | collective-permute-done | bytes 98336 | tf_op jit(solution)/shard_map/ppermute | solution.py:21
  111.3 2.6 fusion.129
  113.9 8.6 %collective-permute-done.2 = bf16[96,512]{0,1:T(8,128)(2,1)S(1)} collective-permute-done((bf16[96,512]{0,1:T(8,128)(2,1)S(1)}, bf16[96,512]{0,1:T(8,128)(2,1)S(1)}, u32[]{:S(2)}, u32[]{:S(2)}) %collective-permute-start.2) | collective-permute-done | bytes 98336 | tf_op jit(solution)/shard_map/ppermute | solution.py:21
  123.2 2.6 fusion.130
  125.8 103.6 %collective-permute-done.3 = bf16[96,512]{0,1:T(8,128)(2,1)S(1)} collective-permute-done((bf16[96,512]{0,1:T(8,128)(2,1)S(1)}, bf16[96,512]{0,1:T(8,128)(2,1)S(1)}, u32[]{:S(2)}, u32[]{:S(2)}) %collective-permute-start.3) | collective-permute-done | bytes 98336 | tf_op jit(solution)/shard_map/ppermute | solution.py:21
  229.9 4.8 collective-permute-start.4
  234.8 3.6 fusion.131
  238.4 65.6 %collective-permute-done.4 = bf16[96,512]{0,1:T(8,128)(2,1)S(1)} collective-permute-done((bf16[96,512]{0,1:T(8,128)(2,1)S(1)}, bf16[96,512]{0,1:T(8,128)(2,1)S(1)}, u32[]{:S(2)}, u32[]{:S(2)}) %collective-permute-start.4) | collective-permute-done | bytes 98336 | tf_op jit(solution)/shard_map/ppermute | solution.py:21
  304.2 3.4 fusion.132
  307.6 4.5 fusion.124
  312.1 12.6 %gather_fusion.1 = bf16[96,96,512]{2,1,0:T(8,128)(2,1)} fusion(bf16[32,4,96,512]{3,2,1,0:T(8,128)(2,1)} %all-to-all-done, s32[96]{0:T(128)S(1)} %reshape.205), kind=kCustom, calls=%fused_computation.1 | custom fusion | bytes 18875136 | tf_op jit(solution)/shard_map/gather | solution.py:95
  324.6 6.6 %fusion.173 = (bf16[12,96,512]{2,1,0:T(8,128)(2,1)S(1)}, bf16[12,96,512]{2,1,0:T(8,128)(2,1)S(1)}, bf16[12,96,512]{2,1,0:T(8,128)(2,1)}, bf16[12,96,512]{2,1,0:T...) fusion(bf16[96,96,512]{2,1,0:T(8,128)(2,1)} %gather_fusion.1), kind=kLoop, calls=%fused_computation.288 | loop fusion | bytes 18874368 | tf_op jit(solution)/shard_map/slice | solution.py:100
  331.3 35.1 %while.81 = (s32[]{:T(128)}, f32[32,512]{1,0:T(8,128)S(1)}, s32[]{:T(128)}, bf16[12,96,512]{2,1,0:T(8,128)(2,1)}, bf16[64,512]{1,0:T(8,128)(2,1)S(1)}, /*index=5*/s32[]{:T(128)}, s32[]{:T(128)}, s32[]{:T(128)}, s32[]{}) while((s32[]{:T(128)}, f32[32,512]{1,0:T(8,128)S(1)}, s32[]{:T(128)}, bf16[12,96,512]{2,1,0:T(8,128)(2,1)}, ...), condition=%wide.region_9.10_spmd, body=%wide.region_6.9_spmd.sunk | while | flops 51854340 | bytes 435855 | solution.py:106
  366.5 36.1 %while.80 = (s32[]{:T(128)}, f32[32,512]{1,0:T(8,128)S(1)}, s32[]{:T(128)}, bf16[12,96,512]{2,1,0:T(8,128)(2,1)}, bf16[64,512]{1,0:T(8,128)(2,1)S(1)}, /*index=5*/s32[]{:T(128)}, s32[]{:T(128)}, s32[]{:T(128)}, s32[]{}) while((s32[]{:T(128)}, f32[32,512]{1,0:T(8,128)S(1)}, s32[]{:T(128)}, bf16[12,96,512]{2,1,0:T(8,128)(2,1)}, ...), condition=%wide.region_5.6_spmd, body=%wide.region_2.5_spmd.sunk | while | flops 51854340 | bytes 435855 | solution.py:106
  404.1 43.1 %while.82 = (s32[]{:T(128)}, f32[32,512]{1,0:T(8,128)}, s32[]{:T(128)}, bf16[12,96,512]{2,1,0:T(8,128)(2,1)}, bf16[64,512]{1,0:T(8,128)(2,1)S(1)}, /*index=5*/s32[]{:T(128)}, s32[]{:T(128)}, s32[]{:T(128)}, s32[]{}) while((s32[]{:T(128)}, f32[32,512]{1,0:T(8,128)}, s32[]{:T(128)}, bf16[12,96,512]{2,1,0:T(8,128)(2,1)}, ...), condition=%wide.region_13.14_spmd, body=%wide.region_10.13_spmd.sunk | while | flops 51854340 | bytes 435855 | solution.py:106
  416.2 2.1 fusion.210
  419.8 2.1 fusion.210
  423.3 2.1 fusion.210
  426.9 2.1 fusion.210
  430.4 2.1 fusion.210
  434.0 2.1 fusion.210
  437.5 2.1 fusion.210
  441.1 2.1 fusion.210
  444.6 2.1 fusion.210
  447.3 36.1 %while.83 = (s32[]{:T(128)}, f32[32,512]{1,0:T(8,128)S(1)}, s32[]{:T(128)}, bf16[12,96,512]{2,1,0:T(8,128)(2,1)}, bf16[64,512]{1,0:T(8,128)(2,1)S(1)}, /*index=5*/s32[]{:T(128)}, s32[]{:T(128)}, s32[]{:T(128)}, s32[]{}) while((s32[]{:T(128)}, f32[32,512]{1,0:T(8,128)S(1)}, s32[]{:T(128)}, bf16[12,96,512]{2,1,0:T(8,128)(2,1)}, ...), condition=%wide.region_17.18_spmd, body=%wide.region_14.17_spmd.sunk | while | flops 51854340 | bytes 435855 | solution.py:106
  483.4 36.8 %while.84 = (s32[]{:T(128)}, f32[32,512]{1,0:T(8,128)S(1)}, s32[]{:T(128)}, bf16[12,96,512]{2,1,0:T(8,128)(2,1)}, bf16[64,512]{1,0:T(8,128)(2,1)S(1)}, /*index=5*/s32[]{:T(128)}, s32[]{:T(128)}, s32[]{:T(128)}, s32[]{}) while((s32[]{:T(128)}, f32[32,512]{1,0:T(8,128)S(1)}, s32[]{:T(128)}, bf16[12,96,512]{2,1,0:T(8,128)(2,1)}, ...), condition=%wide.region_21.22_spmd, body=%wide.region_18.21_spmd.sunk | while | flops 51854340 | bytes 435855 | solution.py:106
  520.3 35.9 %while.85 = (s32[]{:T(128)}, f32[32,512]{1,0:T(8,128)S(1)}, s32[]{:T(128)}, bf16[12,96,512]{2,1,0:T(8,128)(2,1)}, bf16[64,512]{1,0:T(8,128)(2,1)S(1)}, /*index=5*/s32[]{:T(128)}, s32[]{:T(128)}, s32[]{:T(128)}, s32[]{}) while((s32[]{:T(128)}, f32[32,512]{1,0:T(8,128)S(1)}, s32[]{:T(128)}, bf16[12,96,512]{2,1,0:T(8,128)(2,1)}, ...), condition=%wide.region_25.26_spmd, body=%wide.region_22.25_spmd.sunk | while | flops 51854340 | bytes 435855 | solution.py:106
  556.2 15.8 %while.86 = (s32[]{:T(128)}, f32[32,512]{1,0:T(8,128)S(1)}, s32[]{:T(128)}, bf16[12,96,512]{2,1,0:T(8,128)(2,1)S(1)}, bf16[64,512]{1,0:T(8,128)(2,1)S(1)}, /*index=5*/s32[]{:T(128)}, s32[]{:T(128)}, s32[]{:T(128)}, s32[]{}) while((s32[]{:T(128)}, f32[32,512]{1,0:T(8,128)S(1)}, s32[]{:T(128)}, bf16[12,96,512]{2,1,0:T(8,128)(2,1)S(1)}, ...), condition=%wide.region_29.30_spmd, body=%wide.region_26.29_spmd.sunk | while | flops 51854340 | bytes 435855 | solution.py:106
  572.0 15.6 %while.87 = (s32[]{:T(128)}, f32[32,512]{1,0:T(8,128)S(1)}, s32[]{:T(128)}, bf16[12,96,512]{2,1,0:T(8,128)(2,1)S(1)}, bf16[64,512]{1,0:T(8,128)(2,1)S(1)}, /*index=5*/s32[]{:T(128)}, s32[]{:T(128)}, s32[]{:T(128)}, s32[]{}) while((s32[]{:T(128)}, f32[32,512]{1,0:T(8,128)S(1)}, s32[]{:T(128)}, bf16[12,96,512]{2,1,0:T(8,128)(2,1)S(1)}, ...), condition=%wide.region_33.34_spmd, body=%wide.region_30.33_spmd.sunk | while | flops 51854340 | bytes 435855 | solution.py:106
  (287 shorter events, 185.4 us)
Async XLA Ops:
  12.3 7.5 %copy-start = (bf16[64,4096]{1,0:T(8,128)(2,1)S(1)}, bf16[64,4096]{1,0:T(8,128)(2,1)}, u32[]{:S(2)}) copy-start(bf16[64,4096]{1,0:T(8,128)(2,1)} %param.22) | copy-start | bytes 1572868
  12.3 8.0 %copy-start.10 = (bf16[32,4096]{1,0:T(8,128)(2,1)S(1)}, bf16[32,4096]{1,0:T(8,128)(2,1)}, u32[]{:S(2)}) copy-start(bf16[32,4096]{1,0:T(8,128)(2,1)} %param.23) | copy-start | bytes 786436
  12.3 8.0 %copy-start.11 = (s32[4096]{0:T(1024)S(1)}, s32[4096]{0:T(1024)}, u32[]{:S(2)}) copy-start(s32[4096]{0:T(1024)} %param.25) | copy-start | bytes 49156
  12.3 11.8 %copy-start.12 = (s32[256]{0:T(256)S(1)}, s32[256]{0:T(256)}, u32[]{:S(2)}) copy-start(s32[256]{0:T(256)} %param.27) | copy-start | bytes 3076
  12.4 299.7 %all-to-all-start = ((bf16[32,4,96,512]{3,2,1,0:T(8,128)(2,1)}), bf16[32,4,96,512]{3,2,1,0:T(8,128)(2,1)}, u32[]{:S(2)}, u32[]{:S(2)}) async-start(bf16[32,4,96,512]{3,2,1,0:T(8,128)(2,1)} %bitcast.215), calls=%async_computation | async-start | bytes 25165824 | tf_op jit(solution)/shard_map/all_to_all | solution.py:94
  23.6 5.4 collective-permute-start
  29.5 81.0 %collective-permute-start.1 = (bf16[96,512]{0,1:T(8,128)(2,1)S(1)}, bf16[96,512]{0,1:T(8,128)(2,1)S(1)}, u32[]{:S(2)}, u32[]{:S(2)}) collective-permute-start(bf16[96,512]{0,1:T(8,128)(2,1)S(1)} %maximum_maximum_fusion), channel_id=1, source_target_pairs={{0,2},{2,0},{1,3},{3,1},{4,6},{6,4},{5,7},{7,5},{8,10},{10,8},{9,1... | collective-permute-start | bytes 294920 | tf_op jit(solution)/shard_map/ppermute | solution.py:21
  111.0 11.4 %collective-permute-start.2 = (bf16[96,512]{0,1:T(8,128)(2,1)S(1)}, bf16[96,512]{0,1:T(8,128)(2,1)S(1)}, u32[]{:S(2)}, u32[]{:S(2)}) collective-permute-start(bf16[96,512]{0,1:T(8,128)(2,1)S(1)} %maximum_maximum_fusion.1), channel_id=1, source_target_pairs={{0,4},{4,0},{1,5},{5,1},{2,6},{6,2},{3,7},{7,3},{8,12},{12,8},{9,1... | collective-permute-start | bytes 294920 | tf_op jit(solution)/shard_map/ppermute | solution.py:21
  123.0 106.4 %collective-permute-start.3 = (bf16[96,512]{0,1:T(8,128)(2,1)S(1)}, bf16[96,512]{0,1:T(8,128)(2,1)S(1)}, u32[]{:S(2)}, u32[]{:S(2)}) collective-permute-start(bf16[96,512]{0,1:T(8,128)(2,1)S(1)} %maximum_maximum_fusion.2), channel_id=1, source_target_pairs={{0,8},{8,0},{1,9},{9,1},{2,10},{10,2},{3,11},{11,3},{4,12},{12,4},... | collective-permute-start | bytes 294920 | tf_op jit(solution)/shard_map/ppermute | solution.py:21
  229.9 74.1 %collective-permute-start.4 = (bf16[96,512]{0,1:T(8,128)(2,1)S(1)}, bf16[96,512]{0,1:T(8,128)(2,1)S(1)}, u32[]{:S(2)}, u32[]{:S(2)}) collective-permute-start(bf16[96,512]{0,1:T(8,128)(2,1)S(1)} %maximum_maximum_fusion.3), channel_id=1, source_target_pairs={{0,16},{16,0},{1,17},{17,1},{2,18},{18,2},{3,19},{19,3},{4,20},{20... | collective-permute-start | bytes 294920 | tf_op jit(solution)/shard_map/ppermute | solution.py:21
  304.0 3.6 copy-start.13
  324.6 6.6 %copy-start.7 = (f32[32,512]{1,0:T(8,128)S(1)}, f32[32,512]{1,0:T(8,128)}, u32[]{:S(2)}) copy-start(f32[32,512]{1,0:T(8,128)} %get-tuple-element.690) | copy-start | bytes 196612
  324.6 41.8 %copy-start.5 = (f32[32,512]{1,0:T(8,128)S(1)}, f32[32,512]{1,0:T(8,128)}, u32[]{:S(2)}) copy-start(f32[32,512]{1,0:T(8,128)} %get-tuple-element.663) | copy-start | bytes 196612
  366.4 36.2 %copy-start.8 = (f32[32,512]{1,0:T(8,128)}, f32[32,512]{1,0:T(8,128)S(1)}, u32[]{:S(2)}) copy-start(f32[32,512]{1,0:T(8,128)S(1)} %get-tuple-element.227) | copy-start | bytes 196612
  366.4 80.8 %copy-start.3 = (f32[32,512]{1,0:T(8,128)S(1)}, f32[32,512]{1,0:T(8,128)}, u32[]{:S(2)}) copy-start(f32[32,512]{1,0:T(8,128)} %get-tuple-element.744) | copy-start | bytes 196612
  402.6 0.6 copy-start.6
  403.3 80.2 %copy-start.2 = (f32[32,512]{1,0:T(8,128)S(1)}, f32[32,512]{1,0:T(8,128)}, u32[]{:S(2)}) copy-start(f32[32,512]{1,0:T(8,128)} %get-tuple-element.771) | copy-start | bytes 196612
  447.3 73.0 %copy-start.1 = (f32[32,512]{1,0:T(8,128)S(1)}, f32[32,512]{1,0:T(8,128)}, u32[]{:S(2)}) copy-start(f32[32,512]{1,0:T(8,128)} %get-tuple-element.798) | copy-start | bytes 196612
  556.2 31.4 %copy-start.9 = (f32[32,512]{1,0:T(8,128)S(1)}, f32[32,512]{1,0:T(8,128)}, u32[]{:S(2)}) copy-start(f32[32,512]{1,0:T(8,128)} %copy-done.8) | copy-start | bytes 196612
  556.2 31.4 %copy-start.4 = (f32[32,512]{1,0:T(8,128)S(1)}, f32[32,512]{1,0:T(8,128)}, u32[]{:S(2)}) copy-start(f32[32,512]{1,0:T(8,128)} %get-tuple-element.228) | copy-start | bytes 196612
where the time goes:
time: 597 us; the launch traced here: 589 us
  waiting for transfers between devices  257 us (43%)
  matrix products  144 us (24%)
  other arithmetic  70.6 us (12%)
  loops' own time  67.2 us (11%)
  local copies, waits for them, and re-layouts  34.4 us (6%)
  starting transfers between devices  14.4 us (2%)
    ppermute x5, waiting for transfers between devices, from_partner(): return lax.ppermute(block, axis, route)  257 us
    dot_general x102, matrix products, kernel_apply(): return jnp.dot(source_w, kernel_tile, preferred_element_type=jnp.float32)  142 us
    another operation x8, loops' own time, per_device(): lax.fori_loop(0, my_count[leaf_pos], add_slot, own_terms[leaf_pos])  67.2 us
    reduce_sum x97, other arithmetic, kernel_apply(): target_sq = jnp.sum(jnp.square(targets.astype(jnp.float32)), axis=0)  64.9 us
    gather x1, local copies, waits for them, and re-layouts, per_device(): incoming[my_owner.reshape(leaves_dev, NEAR), slot_round.reshape(leaves_de...  12.6 us
  transfers between devices with their start and end apart: 6, of which 4 were waited for; matrix products, arithmetic and copies ran while one was open for 5% of the time, Pallas kernels for 0%

commit v1 on v0

v1 whole, which is shorter than its diff:
```python
import functools
import math

import jax
import jax.numpy as jnp
from jax import lax
from jax.experimental import pallas as pl
from jax.experimental.pallas import tpu as pltpu
from jax.sharding import PartitionSpec as P

D = 64
RHS = 32
LEAF = 512
SKEL = 512
NEAR = 12
ROWS = D + RHS
DEPTH = 256
SCALE2 = 1.0 / (D * math.log(2.0))
SLOTS = 4


def three_parts(x):
    high = x.astype(jnp.bfloat16).astype(jnp.float32)
    rest = x - high
    mid = rest.astype(jnp.bfloat16).astype(jnp.float32)
    low = (rest - mid).astype(jnp.bfloat16).astype(jnp.float32)
    return high, mid, low


def neg_norm_parts(points32):
    norm = jnp.sum(points32 * points32, axis=0, keepdims=True) * (-SCALE2)
    return three_parts(norm)


def tail_rows(parts, first, ones_first, rows):
    row = lax.broadcasted_iota(jnp.int32, (rows, parts[0].shape[1]), 0)
    tail = jnp.where((row >= ones_first) & (row < ones_first + 3), 1.0, 0.0)
    for step, part in enumerate(parts):
        tail = jnp.where(row == first + step, part, tail)
    return tail


def target_side(points):
    points32 = points.astype(jnp.float32)
    parts = three_parts(points32 * (2.0 * SCALE2))
    tail = tail_rows(neg_norm_parts(points32), 3, 0, DEPTH - 3 * D)
    return jnp.concatenate([*parts, tail], axis=0).T.astype(jnp.bfloat16)


def source_side(points):
    tail = tail_rows(neg_norm_parts(points.astype(jnp.float32)), 0, 3, DEPTH - 3 * D)
    return jnp.concatenate([points, points, points, tail.astype(jnp.bfloat16)], axis=0)


def tile_term(target, points, weights):
    exponent = jnp.dot(target, source_side(points), preferred_element_type=jnp.float32)
    tile = jnp.exp2(exponent).astype(jnp.bfloat16)
    return lax.dot_general(
        tile, weights, (((1,), (1,)), ((), ())), preferred_element_type=jnp.float32
    )


def local_kernel(depth_count, far_scale, points_ref, weights_ref, nodes_ref, self_ref, far_ref):
    points = points_ref[...]
    target = target_side(points)
    self_ref[...] = tile_term(target, points, weights_ref[...]).T
    total = jnp.zeros((LEAF, RHS), jnp.float32)
    for level in range(depth_count):
        total = total + tile_term(target, nodes_ref[level, :D, :], nodes_ref[level, D:, :])
    far_ref[...] = total.T * far_scale


def near_kernel(leaves_dev, near_scale, owner_ref, place_ref, start_ref, points_ref, self_ref,
                blocks_ref, out_ref, held, sems):
    total_items = start_ref[leaves_dev]

    def fetch(item):
        slot = lax.rem(item, SLOTS)
        column = pl.multiple_of(place_ref[item] * LEAF, LEAF)
        return pltpu.make_async_copy(
            blocks_ref.at[owner_ref[item], :, pl.ds(column, LEAF)], held.at[slot], sems.at[slot]
        )

    for ahead in range(SLOTS - 1):
        @pl.when(ahead < total_items)
        def _():
            fetch(ahead).start()

    def leaf_step(leaf, carry):
        columns = pl.ds(pl.multiple_of(leaf * LEAF, LEAF), LEAF)
        target = target_side(points_ref[:, columns])

        def item_step(item, running):
            @pl.when(item + SLOTS - 1 < total_items)
            def _():
                fetch(item + SLOTS - 1).start()
            fetch(item).wait()
            slot = lax.rem(item, SLOTS)
            return running + tile_term(target, held[slot, :D, :], held[slot, D:, :])

        total = lax.fori_loop(
            start_ref[leaf], start_ref[leaf + 1], item_step, jnp.zeros((LEAF, RHS), jnp.float32)
        )
        out_ref[:, columns] = (total.T + self_ref[:, columns]) * near_scale
        return carry

    lax.fori_loop(0, leaves_dev, leaf_step, 0)


def fold_child(nodes):
    half = nodes.shape[-1] // 2
    folded = nodes[..., D:, :half].astype(jnp.float32) + nodes[..., D:, half:].astype(jnp.float32)
    return jnp.concatenate([nodes[..., :D, :half], folded.astype(jnp.bfloat16)], axis=-2)


def sibling_nodes(nodes, my_index, depth_count):
    found = []
    for level in range(depth_count):
        found.append(lax.dynamic_index_in_dim(nodes, (my_index >> level) ^ 1, 0, keepdims=False))
        if level + 1 < depth_count:
            child = fold_child(nodes)
            nodes = jnp.concatenate([child[0::2], child[1::2]], axis=-1)
    return jnp.stack(found)


def per_device(points, weights, skel_index, assign, near_leaf, near_count):
    n_dev = lax.axis_size("leaf")
    my_index = lax.axis_index("leaf")
    depth_count = n_dev.bit_length() - 1
    p_dev = points.shape[1]
    leaves_dev = p_dev // LEAF

    member = (assign[None, :] == jnp.arange(SKEL, dtype=jnp.int32)[:, None]).astype(jnp.bfloat16)
    base_weights = lax.dot_general(
        weights, member, (((1,), (1,)), ((), ())), preferred_element_type=jnp.float32
    )
    base_node = jnp.concatenate([points[:, skel_index], base_weights.astype(jnp.bfloat16)], axis=0)
    stacked = jnp.concatenate([points, weights], axis=0)
    base_node, stacked = lax.optimization_barrier((base_node, stacked))
    nodes = lax.all_gather(base_node, "leaf")
    blocks = lax.all_gather(stacked, "leaf")

    slot_count = leaves_dev * NEAR
    my_leaf = lax.dynamic_slice_in_dim(near_leaf, my_index * leaves_dev, leaves_dev).reshape(-1)
    my_count = lax.dynamic_slice_in_dim(near_count, my_index * leaves_dev, leaves_dev)
    before = jnp.arange(leaves_dev + 1)[:, None] > jnp.arange(leaves_dev)[None, :]
    start = jnp.sum(jnp.where(before, my_count[None, :], 0), axis=1).astype(jnp.int32)
    slot = jnp.arange(slot_count, dtype=jnp.int32)
    live = slot % NEAR < jnp.repeat(my_count, NEAR)
    spot = jnp.where(live, jnp.repeat(start[:-1], NEAR) + slot % NEAR, slot_count)
    chosen = spot[None, :] == slot[:, None]
    item_leaf = jnp.sum(jnp.where(chosen, my_leaf[None, :], 0), axis=1).astype(jnp.int32)

    siblings = sibling_nodes(nodes, my_index, depth_count)
    tile_flops = 2 * LEAF * LEAF * (DEPTH + 256)
    column_block = lambda rows: pl.BlockSpec((rows, LEAF), lambda leaf: (0, leaf))
    self_term, far_field = pl.pallas_call(
        functools.partial(local_kernel, depth_count, 4.0 / math.sqrt(p_dev * n_dev)),
        grid=(leaves_dev,),
        in_specs=[
            column_block(D),
            column_block(RHS),
            pl.BlockSpec((depth_count, ROWS, SKEL), lambda leaf: (0, 0, 0)),
        ],
        out_specs=[column_block(RHS), column_block(RHS)],
        out_shape=[jax.ShapeDtypeStruct((RHS, p_dev), jnp.float32)] * 2,
        compiler_params=pltpu.CompilerParams(vmem_limit_bytes=48 * 2**20),
        cost_estimate=pl.CostEstimate(
            flops=leaves_dev * (depth_count + 1) * tile_flops,
            bytes_accessed=4 * 2**20,
            transcendentals=leaves_dev * (depth_count + 1) * LEAF * LEAF,
        ),
        name="local_and_far",
    )(points, weights, siblings)

    whole = pl.BlockSpec(memory_space=pltpu.VMEM)
    scalars = pl.BlockSpec(memory_space=pltpu.SMEM)
    near_field = pl.pallas_call(
        functools.partial(near_kernel, leaves_dev, 4.0 / math.sqrt(LEAF * (NEAR + 1))),
        in_specs=[scalars, scalars, scalars, whole, whole, pl.BlockSpec(memory_space=pl.ANY)],
        out_specs=whole,
        out_shape=jax.ShapeDtypeStruct((RHS, p_dev), jnp.float32),
        scratch_shapes=[
            pltpu.VMEM((SLOTS, ROWS, LEAF), jnp.bfloat16),
            pltpu.SemaphoreType.DMA((SLOTS,)),
        ],
        compiler_params=pltpu.CompilerParams(vmem_limit_bytes=48 * 2**20),
        cost_estimate=pl.CostEstimate(
            flops=slot_count * tile_flops,
            bytes_accessed=slot_count * ROWS * LEAF * 2,
            transcendentals=slot_count * LEAF * LEAF,
        ),
        name="near_blocks",
    )(item_leaf // leaves_dev, item_leaf % leaves_dev, start, points, self_term, blocks)
    return (near_field, far_field)


def solution(mesh):
    return jax.shard_map(
        per_device,
        mesh=mesh,
        in_specs=(P(None, "leaf"), P(None, "leaf"), P("leaf"), P("leaf"), P(), P()),
        out_specs=(P(None, "leaf"), P(None, "leaf")),
        check_vma=False,
    )
```

time: 597 us -> 286 us (0.48); the launches traced: 589 us -> 286 us
  matrix products: 144 us -> 1.53 us
  other arithmetic: 70.6 us -> 3.11 us
  loops' own time: 67.2 us -> 0 us
  Pallas kernels: 0 us -> 65.7 us
  waiting for transfers between devices: 257 us -> 194 us
  local copies, waits for them, and re-layouts: 34.4 us -> 6.95 us
  starting transfers between devices: 14.4 us -> 0.08 us
  between operations: 1.23 us -> 14.4 us
    ppermute x5 -> x0, waiting for transfers between devices: 257 us -> none  [from_partner(): return lax.ppermute(block, axis, route)]
    all_gather x0 -> x2, waiting for transfers between devices: none -> 193 us  [the longest x1 133 us: per_device(): blocks = lax.all_gather(stacked, 'leaf')]
    dot_general x102 -> x0, matrix products: 142 us -> none  [kernel_apply(): return jnp.dot(source_w, kernel_tile, preferred_element_type=jnp.float32)]
    another operation x8 -> x0, loops' own time: 67.2 us -> none  [per_device(): lax.fori_loop(0, my_count[leaf_pos], add_slot, own_terms[leaf_pos])]
    reduce_sum x104 -> x2, other arithmetic: 66 us -> 0.2 us  [the longest x1 0.11 us: per_device(): jnp.sum(jnp.where(chosen, my_leaf[None, :], 0), axis=1).astype(jnp.int32)]
    pallas_call x0 -> x2, Pallas kernels: none -> 65.7 us  [the longest x1 46.8 us: per_device(): pl.pallas_call(functools.partial(near_kernel, leaves_dev, 4.0 / math.sqrt...]
    gather x2 -> x0, local copies, waits for them, and re-layouts: 20.7 us -> none  [the longest x1 12.6 us: per_device(): incoming[my_owner.reshape(leaves_dev, NEAR), slot_round.reshape(leaves_de...]
    all_to_all x1 -> x0, starting transfers between devices: 7.45 us -> none  [per_device(): lax.all_to_all(outgoing, 'leaf', split_axis=0, concat_axis=0, tiled=True)]
  transfers between devices with their start and end apart: 6 -> 2, of which waited for: 4 -> 2; matrix products, arithmetic and copies ran while one was open for 5% -> 2% of each run, Pallas kernels for 0% -> 7%
where the time goes in v1:
time: 286 us
  waiting for transfers between devices  194 us (68%)
  Pallas kernels  65.7 us (23%)
  between operations  14.4 us (5%)
  local copies, waits for them, and re-layouts  6.95 us (2%)
  other arithmetic  3.11 us (1%)
    all_gather x1, waiting for transfers between devices, per_device(): blocks = lax.all_gather(stacked, 'leaf')  133 us
    all_gather x1, waiting for transfers between devices, per_device(): nodes = lax.all_gather(base_node, 'leaf')  60.1 us
    pallas_call x1, Pallas kernels, per_device(): pl.pallas_call(functools.partial(near_kernel, leaves_dev, 4.0 / math.sqrt...  46.8 us
    pallas_call x1, Pallas kernels, per_device(): pl.pallas_call(functools.partial(local_kernel, depth_count, 4.0 / math.sq...  18.9 us
  transfers between devices with their start and end apart: 2, of which 2 were waited for; matrix products, arithmetic and copies ran while one was open for 2% of the time, Pallas kernels for 7%

profile of v1, /device:TPU:0, one launch (start us, length us, event | category | flops | bytes accessed | tf_op | source)
XLA Modules:
  0.0 285.5 jit_solution(10763490684359711930)
XLA Ops:
  7.2 0.0 all-gather.5.cloned.1.call-start
  7.3 1.6 copy.17
  8.9 0.9 pad_maximum_fusion.1
  9.9 1.5 fusion.3
  11.4 0.1 copy.18
  11.5 1.3 gather_fusion
  12.9 0.1 pad_maximum_fusion.5
  13.0 0.7 copy.19
  13.8 0.0 all-gather.7.cloned.1.call-start
  13.8 0.7 all-gather.7.cloned.1.call-update
  14.5 0.1 dynamic_slice.26
  14.6 0.1 select_reduce_fusion.1.start_ref
  14.7 0.1 broadcast_in_dim.49
  14.8 0.1 reshape.34
  14.9 0.1 broadcast_in_dim.46
  14.9 0.1 reshape.33
  15.0 0.1 constant_dynamic-slice_fusion
  15.1 0.1 copy.16
  15.2 0.1 broadcast_in_dim.51
  15.3 0.1 select_reduce_fusion
  15.4 60.1 %all-gather.5.cloned.1.call-done = bf16[3072,512]{1,0:T(8,128)(2,1)} async-done(((bf16[96,512]{1,0:T(8,128)(2,1)}), bf16[3072,512]{1,0:T(8,128)(2,1)}) %all-gather.5.cloned.1.call-update) | async-done | bytes 3145744 | tf_op jit(solution)/shard_map/all_gather | solution.py:140
  75.5 1.3 slice.86
  76.9 1.4 add_convert_fusion
  78.3 0.1 pad_maximum_fusion
  78.4 0.1 fusion.12
  78.6 0.1 add_convert_fusion.1
  78.7 0.1 pad_maximum_fusion.2
  78.7 0.1 fusion.13
  79.0 0.9 dynamic-slice_dynamic-update-slice_fusion
  80.0 18.9 %local_and_far.1 = (f32[32,4096]{1,0:T(8,128)S(1)}, f32[32,4096]{1,0:T(8,128)}) custom-call(bf16[64,4096]{1,0:T(8,128)(2,1)S(1)} %copy-done.1, bf16[32,4096]{1,0:T(8,128)(2,1)S(1)} %copy-done.2, bf16[5,96,512]{2,1,0:T(8,128)(2,1)S(1)} %fusion.9.nodes_ref), custom_call_target="tpu_custom_call" | custom-call | flops 12884901888 | bytes 4194304 | tf_op jit(solution)/shard_map/local_and_far/pallas_call | solution.py:157
  99.0 132.9 %all-gather.7.cloned.1.call-done = bf16[3072,4096]{1,0:T(8,128)(2,1)} async-done(((bf16[96,4096]{1,0:T(8,128)(2,1)}), bf16[3072,4096]{1,0:T(8,128)(2,1)}) %all-gather.7.cloned.1.call-update) | async-done | bytes 25165840 | tf_op jit(solution)/shard_map/all_gather | solution.py:141
  231.9 46.8 %near_blocks.1 = f32[32,4096]{1,0:T(8,128)} custom-call(s32[96]{0:T(128)S(1)} %get-tuple-element.19.owner_ref, s32[96]{0:T(128)S(1)} %get-tuple-element.18.place_ref, s32[9]{0:T(128)S(1)} %select_reduce_fusion.1.start_ref, bf16[64,4096]{1,0:T(8,128)(2,1)S(1)} %copy-done.1, f32[32,4096]{1,0:T(8,128)S(1)} %get-tuple-element.7.self_ref, ...), custom_call_target="tpu_custom_call" | custom-call | flops 25769803776 | bytes 9437184 | tf_op jit(solution)/shard_map/near_blocks/pallas_call | solution.py:178
  (30 shorter events, 0.3 us)
Async XLA Ops:
  7.2 7.9 %copy-start = (s32[256,12]{0,1:T(8,128)S(1)}, s32[256,12]{0,1:T(8,128)}, u32[]{:S(2)}) copy-start(s32[256,12]{0,1:T(8,128)} %param.10) | copy-start | bytes 36868
  7.2 1.7 copy-start.1
  7.2 1.7 copy-start.3
  7.2 1.7 copy-start.2
  7.2 2.6 copy-start.4
  7.2 68.3 %all-gather.5.cloned.1.call-start = ((), (), s32[]{:S(2)}) async-start(), calls=%async_computation | async-start | bytes 3244032 | tf_op jit(solution)/shard_map/all_gather | solution.py:140
  11.4 3.2 %copy-start.5 = (s32[256]{0:T(256)S(1)}, s32[256]{0:T(256)}, u32[]{:S(2)}) copy-start(s32[256]{0:T(256)} %param.11) | copy-start | bytes 3076
  13.8 218.1 %all-gather.7.cloned.1.call-start = ((), (), s32[]{:S(2)}) async-start(), calls=%async_computation.1 | async-start | bytes 25952256 | tf_op jit(solution)/shard_map/all_gather | solution.py:141
Sparse Core Ops, SparseCore 0:
  13.9 61.6 all-gather.4
  78.4 153.4 all-gather.6

commit v2 on v1

--- a/solution.py
+++ b/solution.py
@@ -17,6 +17,7 @@
 DEPTH = 256
 SCALE2 = 1.0 / (D * math.log(2.0))
 SLOTS = 4
+FITS = 32 * 2**20
 
 
 def three_parts(x):
@@ -107,6 +108,327 @@
     lax.fori_loop(0, leaves_dev, leaf_step, 0)
 
 
+def merged(mine, sibling, upper_bit):
+    half = SKEL // 2
+    parts = []
+    for node in (mine, sibling):
+        weights = node[D:, :half].astype(jnp.float32) + node[D:, half:].astype(jnp.float32)
+        parts.append(
+            jnp.concatenate([node[:D, :half].astype(jnp.float32), weights], axis=0)
+        )
+    lower = jnp.where(upper_bit == 0, parts[0], parts[1])
+    upper = jnp.where(upper_bit == 0, parts[1], parts[0])
+    return jnp.concatenate([lower, upper], axis=1).astype(jnp.bfloat16)
+
+
+def fused_kernel(n_dev, caps, near_scale, far_scale, item_ref, spot_ref, leaves_ref, base_ref,
+                 near_ref, far_ref, own, beside, below, across, targets, results, mine, sibling,
+                 recv, send_x, send_y, send_core, send_up, send_down, node_send, node_recv,
+                 local_sem):
+    planes = n_dev // 8
+    depth_count = n_dev.bit_length() - 1
+    leaves_dev = leaves_ref.shape[0]
+    half = leaves_dev // 2
+    cap = max(caps)
+    held = (own, beside, below, across)
+    me = lax.axis_index("leaf")
+    bits = [(me // 2**level) % 2 for level in range(depth_count)]
+    partners = [me + (1 - 2 * bits[level]) * 2**level for level in range(depth_count)]
+    core, plane = bits[0], me // 8
+    core_dev, x_dev, y_dev = partners[:3]
+    up_dev, down_dev = me + 8, me - 8
+
+    barrier = pltpu.get_barrier_semaphore()
+
+    def greet(device):
+        pl.semaphore_signal(
+            barrier, inc=1, device_id=(device,), device_id_type=pl.DeviceIdType.MESH
+        )
+
+    for device in [core_dev, x_dev, y_dev] + partners[4:]:
+        greet(device)
+
+    @pl.when(plane < planes - 1)
+    def _():
+        greet(up_dev)
+
+    @pl.when(plane > 0)
+    def _():
+        greet(down_dev)
+
+    keep = pltpu.make_async_copy(leaves_ref, own.at[plane * 2 + core], local_sem)
+    keep.start()
+    keep.wait()
+    pl.semaphore_wait(
+        barrier,
+        3 + len(partners[4:]) + jnp.where(plane < planes - 1, 1, 0) + jnp.where(plane > 0, 1, 0),
+    )
+
+    def copy(source, target, at, side, part, send_sem, device):
+        piece = pl.ds(part * half, half)
+        return pltpu.make_async_remote_copy(
+            src_ref=held[source].at[at * 2 + side, piece],
+            dst_ref=held[target].at[at * 2 + side, piece],
+            send_sem=send_sem,
+            recv_sem=recv.at[target, at * 2 + side, part],
+            device_id=(device,),
+            device_id_type=pl.DeviceIdType.MESH,
+        )
+
+    def to_core(column, at, part):
+        return copy(column, column, at, core, part, send_core.at[column, at, part], core_dev)
+
+    def to_x(column, at, part):
+        row = part if column == 0 else 2
+        return copy(column, column + 1, at, core, part, send_x.at[row, at], x_dev)
+
+    def to_y(column, at, part):
+        row = part if column == 0 else 2
+        return copy(column, column + 2, at, core, part, send_y.at[row, at], y_dev)
+
+    def to_up(at, part):
+        return copy(0, 0, at, core, part, send_up.at[at, part], up_dev)
+
+    def to_down(at, part):
+        return copy(0, 0, at, core, part, send_down.at[at, part], down_dev)
+
+    def arrived(column, at, side, part):
+        copy(column, column, at, side, part, send_core.at[column, at, part], core_dev).wait_recv()
+
+    def spread(at, part):
+        to_x(0, at, part).start()
+        to_y(0, at, part).start()
+        to_core(0, at, part).start()
+
+    def line_step(step):
+        for part in range(2):
+            @pl.when(plane - step >= 0)
+            def _():
+                arrived(0, plane - step, core, part)
+
+                @pl.when(plane < planes - 1)
+                def _():
+                    to_up(plane - step, part).start()
+                spread(plane - step, part)
+
+            @pl.when(plane + step < planes)
+            def _():
+                arrived(0, plane + step, core, part)
+
+                @pl.when(plane > 0)
+                def _():
+                    to_down(plane + step, part).start()
+                spread(plane + step, part)
+
+    def at_distance(step, action):
+        if step == 0:
+            action(plane)
+            return
+
+        @pl.when(plane - step >= 0)
+        def _():
+            action(plane - step)
+
+        @pl.when(plane + step < planes)
+        def _():
+            action(plane + step)
+
+    def side_step(step):
+        def action(at):
+            for part in range(2):
+                for column in (1, 2):
+                    arrived(column, at, core, part)
+                    if column == 1 and part == 0:
+                        to_y(column, at, part).start()
+                    if column == 2 and part == 1:
+                        to_x(column, at, part).start()
+                    to_core(column, at, part).start()
+        at_distance(step, action)
+
+    def across_step(step):
+        def action(at):
+            for part in range(2):
+                arrived(3, at, core, part)
+                to_core(3, at, part).start()
+        at_distance(step, action)
+
+    def node_copy(level):
+        return pltpu.make_async_remote_copy(
+            src_ref=mine.at[level],
+            dst_ref=sibling.at[level],
+            send_sem=node_send.at[level],
+            recv_sem=node_recv.at[level],
+            device_id=(partners[level],),
+            device_id_type=pl.DeviceIdType.MESH,
+        )
+
+    def columns(leaf):
+        return pl.ds(pl.multiple_of(leaf * LEAF, LEAF), LEAF)
+
+    def self_leaf(leaf, carry):
+        target = target_side(leaves_ref[leaf, :D, :])
+        targets[leaf] = target
+        near_ref[:, columns(leaf)] = tile_term(
+            target, leaves_ref[leaf, :D, :], leaves_ref[leaf, D:, :]
+        ).T
+        far_ref[:, columns(leaf)] = jnp.zeros((RHS, LEAF), jnp.float32)
+        return carry
+
+    def far_levels(first, last):
+        def item(index, carry):
+            level = first + index // leaves_dev
+            leaf = index % leaves_dev
+            term = tile_term(targets[leaf], sibling[level, :D, :], sibling[level, D:, :])
+            far_ref[:, columns(leaf)] += term.T
+            return carry
+        lax.fori_loop(0, (last - first) * leaves_dev, item, 0)
+
+    def next_node(level):
+        node_copy(level).wait_recv()
+        if level + 1 < depth_count:
+            mine[level + 1] = merged(mine[level], sibling[level], bits[level])
+            node_copy(level + 1).start()
+
+    def near_column(column):
+        for at in range(planes):
+            for part in range(2):
+                arrived(column, at, 1 - core, part)
+
+        def item(index, carry):
+            spot = column * cap + index
+            target, place, leaf = item_ref[0, spot], item_ref[1, spot], item_ref[2, spot]
+            block = held[column][place, leaf]
+            results[spot] = tile_term(targets[target], block[:D], block[D:]).T
+            return carry
+        lax.fori_loop(0, caps[column], item, 0)
+
+    mine[0] = base_ref[...]
+    node_copy(0).start()
+    for part in range(2):
+        @pl.when(plane < planes - 1)
+        def _():
+            to_up(plane, part).start()
+
+        @pl.when(plane > 0)
+        def _():
+            to_down(plane, part).start()
+        spread(plane, part)
+    results[4 * cap] = jnp.zeros((RHS, LEAF), jnp.float32)
+    lax.fori_loop(0, leaves_dev, self_leaf, 0)
+    early = min(3, depth_count)
+    for level in range(early):
+        next_node(level)
+    far_levels(0, early)
+    line_step(1)
+    side_step(0)
+    for level in range(early, depth_count):
+        next_node(level)
+    far_levels(early, depth_count)
+    for step in range(2, planes):
+        line_step(step)
+        side_step(step - 1)
+    near_column(0)
+    side_step(planes - 1)
+    near_column(1)
+    near_column(2)
+    for step in range(planes):
+        across_step(step)
+    near_column(3)
+
+    def finish(leaf, carry):
+        total = near_ref[:, columns(leaf)]
+        for slot in range(NEAR):
+            total = total + results[spot_ref[leaf * NEAR + slot]]
+        near_ref[:, columns(leaf)] = total * near_scale
+        far_ref[:, columns(leaf)] = far_ref[:, columns(leaf)] * far_scale
+        return carry
+    lax.fori_loop(0, leaves_dev, finish, 0)
+
+    for level in range(depth_count):
+        node_copy(level).wait_send()
+    for at in range(planes):
+        for part in range(2):
+            to_x(0, at, part).wait_send()
+            to_y(0, at, part).wait_send()
+            for column in range(4):
+                to_core(column, at, part).wait_send()
+
+            @pl.when((plane < planes - 1) & (plane >= at))
+            def _():
+                to_up(at, part).wait_send()
+
+            @pl.when((plane > 0) & (plane <= at))
+            def _():
+                to_down(at, part).wait_send()
+        to_y(1, at, 0).wait_send()
+        to_x(2, at, 1).wait_send()
+
+
+def fused(leaf_blocks, base_node, near_leaf, near_count, n_dev, my_index):
+    leaves_dev = leaf_blocks.shape[0]
+    p_dev = leaves_dev * LEAF
+    slot_count = leaves_dev * NEAR
+    depth_count = n_dev.bit_length() - 1
+    planes = n_dev // 8
+    column_devs = 2 * planes
+    runs = [min(n_dev - 1, slot_count - at) for at in range(0, slot_count, n_dev - 1)]
+    caps = [sum(min(run, column_devs - (column == 0)) for run in runs) for column in range(4)]
+    cap = max(caps)
+
+    my_leaf = lax.dynamic_slice_in_dim(near_leaf, my_index * leaves_dev, leaves_dev).reshape(-1)
+    my_count = lax.dynamic_slice_in_dim(near_count, my_index * leaves_dev, leaves_dev)
+    slot = jnp.arange(slot_count, dtype=jnp.int32)
+    live = slot % NEAR < jnp.repeat(my_count, NEAR)
+    owner = my_leaf // leaves_dev
+    column = (owner // 2 % 4) ^ (my_index // 2 % 4)
+    earlier = (slot[None, :] < slot[:, None]) & live[None, :] & (column[None, :] == column[:, None])
+    rank = jnp.sum(earlier.astype(jnp.int32), axis=1)
+    spot = jnp.where(live, column * cap + rank, 4 * cap).astype(jnp.int32)
+    fields = jnp.stack([slot // NEAR, owner // 8 * 2 + owner % 2, my_leaf % leaves_dev])
+    chosen = spot[None, :] == jnp.arange(4 * cap, dtype=jnp.int32)[:, None]
+    items = jnp.sum(jnp.where(chosen[None], fields[:, None, :], 0), axis=2).astype(jnp.int32)
+
+    tiles = leaves_dev * (depth_count + 1) + sum(caps)
+    whole = pl.BlockSpec(memory_space=pltpu.VMEM)
+    scalars = pl.BlockSpec(memory_space=pltpu.SMEM)
+    dma = pltpu.SemaphoreType.DMA
+    column_buffer = pltpu.VMEM((column_devs, leaves_dev, ROWS, LEAF), jnp.bfloat16)
+    return pl.pallas_call(
+        functools.partial(
+            fused_kernel, n_dev, tuple(caps), 4.0 / math.sqrt(LEAF * (NEAR + 1)),
+            4.0 / math.sqrt(p_dev * n_dev),
+        ),
+        in_specs=[scalars, scalars, whole, whole],
+        out_specs=[whole, whole],
+        out_shape=[jax.ShapeDtypeStruct((RHS, p_dev), jnp.float32)] * 2,
+        scratch_shapes=[
+            column_buffer, column_buffer, column_buffer, column_buffer,
+            pltpu.VMEM((leaves_dev, LEAF, DEPTH), jnp.bfloat16),
+            pltpu.VMEM((4 * cap + 1, RHS, LEAF), jnp.float32),
+            pltpu.VMEM((depth_count, ROWS, SKEL), jnp.bfloat16),
+            pltpu.VMEM((depth_count, ROWS, SKEL), jnp.bfloat16),
+            dma((4, column_devs, 2)),
+            dma((3, planes)),
+            dma((3, planes)),
+            dma((4, planes, 2)),
+            dma((planes, 2)),
+            dma((planes, 2)),
+            dma((depth_count,)),
+            dma((depth_count,)),
+            dma,
+        ],
+        compiler_params=pltpu.CompilerParams(
+            collective_id=0, has_side_effects=True, vmem_limit_bytes=56 * 2**20
+        ),
+        cost_estimate=pl.CostEstimate(
+            flops=tiles * 2 * LEAF * LEAF * (DEPTH + 256),
+            bytes_accessed=4 * 2**20,
+            transcendentals=tiles * LEAF * LEAF,
+        ),
+        name="exchange_and_tiles",
+    )(items, spot, leaf_blocks, base_node)
+
+
 def fold_child(nodes):
     half = nodes.shape[-1] // 2
     folded = nodes[..., D:, :half].astype(jnp.float32) + nodes[..., D:, half:].astype(jnp.float32)
@@ -136,6 +458,9 @@
     )
     base_node = jnp.concatenate([points[:, skel_index], base_weights.astype(jnp.bfloat16)], axis=0)
     stacked = jnp.concatenate([points, weights], axis=0)
+    if n_dev >= 16 and n_dev * stacked.size * 2 <= FITS:
+        leaf_blocks = stacked.reshape(ROWS, leaves_dev, LEAF).transpose(1, 0, 2)
+        return fused(leaf_blocks, base_node, near_leaf, near_count, n_dev, my_index)
     base_node, stacked = lax.optimization_barrier((base_node, stacked))
     nodes = lax.all_gather(base_node, "leaf")
     blocks = lax.all_gather(stacked, "leaf")

time: 286 us -> 190 us (0.66)
  waiting for transfers between devices: 194 us -> 0 us
  Pallas kernels: 65.7 us -> 177 us
  between operations: 14.4 us -> 0.78 us
    all_gather x2 -> x0, waiting for transfers between devices: 193 us -> none  [the longest x1 133 us: per_device(): blocks = lax.all_gather(stacked, 'leaf')]
    pallas_call x2 -> x1, Pallas kernels: 65.7 us -> 177 us  [fused(): pl.pallas_call(functools.partial(fused_kernel, n_dev, tuple(caps), 4.0 /...]
  transfers between devices with their start and end apart: 2 -> 0, of which waited for: 2 -> 0; matrix products, arithmetic and copies ran while one was open for 2% -> 0% of each run, Pallas kernels for 7% -> 0%
where the time goes in v2:
time: 190 us
  Pallas kernels  177 us (93%)
  local copies, waits for them, and re-layouts  7.76 us (4%)
  other arithmetic  2.9 us (2%)
    pallas_call x1, Pallas kernels, fused(): pl.pallas_call(functools.partial(fused_kernel, n_dev, tuple(caps), 4.0 /...  177 us
    unnamed x17, local copies, waits for them, and re-layouts  4.14 us

profile of v2, /device:TPU:0, one launch (start us, length us, event | category | flops | bytes accessed | tf_op | source)
XLA Modules:
  0.0 189.6 jit_solution(12754495991767941011)
XLA Ops:
  0.6 0.0 copy-start
  0.7 0.7 copy-done
  1.4 0.1 constant_dynamic-slice_fusion
  1.4 0.1 copy.17
  1.5 0.1 reshape.368
  1.6 0.8 dynamic_slice.6
  2.4 0.1 broadcast_in_dim.21
  2.5 0.1 reshape.367
  2.6 0.2 convert_reduce_fusion
  2.8 0.0 copy-start.4
  2.8 0.1 iota_compare_fusion.6
  2.9 0.1 reshape.369
  3.0 0.7 select_reduce_fusion.item_ref
  3.7 1.2 pad_maximum_fusion
  4.9 0.0 copy-start.1
  4.9 1.0 copy.24
  5.8 0.0 copy-done.4
  5.8 0.0 copy-start.5
  5.8 0.2 copy-done.1
  6.1 0.5 copy.20
  6.5 0.0 copy-done.5
  6.6 1.3 gather_fusion
  7.9 0.1 copy.21
  8.0 0.0 copy-done.3
  8.0 0.0 copy-done.6
  8.0 1.5 fusion.3
  9.6 0.7 pad_maximum_fusion.1.base_ref
  10.2 176.6 %exchange_and_tiles.1 = (f32[32,4096]{1,0:T(8,128)}, f32[32,4096]{1,0:T(8,128)}) custom-call(s32[3,108]{1,0:T(4,128)} %select_reduce_fusion.item_ref, s32[96]{0:T(128)} %copy-done.4, bf16[8,96,512]{2,1,0:T(8,128)(2,1)} %bitcast.12, bf16[96,512]{1,0:T(8,128)(2,1)} %pad_maximum_fusion.1.base_ref), custom_call_target="tpu_custom_call" | custom-call | flops 41070624768 | bytes 4194304 | tf_op jit(solution)/shard_map/exchange_and_tiles/pallas_call | solution.py:396
  186.9 0.0 copy-start.2
  186.9 1.9 %copy.27 = f32[32,4096]{1,0:T(8,128)} copy(f32[32,4096]{1,0:T(8,128)} %get-tuple-element.7) | data formatting | bytes 1048576
  188.8 0.0 copy-done.2
  188.8 0.8 copy.28
  (9 shorter events, 0.1 us)
Async XLA Ops:
  0.6 0.7 copy-start
  2.8 3.1 %copy-start.4 = (s32[96]{0:T(128)}, s32[96]{0:T(128)S(1)}, u32[]{:S(2)}) copy-start(s32[96]{0:T(128)S(1)} %add_select_fusion.spot_ref) | copy-start | bytes 1156
  4.9 1.2 copy-start.1
  5.8 0.7 copy-start.5
  6.1 2.0 %copy-start.3 = (bf16[32,4096]{1,0:T(8,128)(2,1)S(1)}, bf16[32,4096]{1,0:T(8,128)(2,1)}, u32[]{:S(2)}) copy-start(bf16[32,4096]{1,0:T(8,128)(2,1)} %param.7) | copy-start | bytes 786436
  6.1 2.0 %copy-start.6 = (s32[4096]{0:T(1024)S(1)}, s32[4096]{0:T(1024)}, u32[]{:S(2)}) copy-start(s32[4096]{0:T(1024)} %param.9) | copy-start | bytes 49156
  186.9 1.9 %copy-start.2 = (f32[32,4096]{1,0:T(8,128)S(1)}, f32[32,4096]{1,0:T(8,128)}, u32[]{:S(2)}) copy-start(f32[32,4096]{1,0:T(8,128)} %get-tuple-element.8) | copy-start | bytes 1572868

commit v3 on v1

--- a/solution.py
+++ b/solution.py
@@ -17,6 +17,7 @@
 DEPTH = 256
 SCALE2 = 1.0 / (D * math.log(2.0))
 SLOTS = 4
+PER_PAIR = 4
 
 
 def three_parts(x):
@@ -107,6 +108,323 @@
     lax.fori_loop(0, leaves_dev, leaf_step, 0)
 
 
+def merged(mine, sibling, upper_bit):
+    half = SKEL // 2
+    parts = []
+    for node in (mine, sibling):
+        weights = node[D:, :half].astype(jnp.float32) + node[D:, half:].astype(jnp.float32)
+        parts.append(
+            jnp.concatenate([node[:D, :half].astype(jnp.float32), weights], axis=0)
+        )
+    lower = jnp.where(upper_bit == 0, parts[0], parts[1])
+    upper = jnp.where(upper_bit == 0, parts[1], parts[0])
+    return jnp.concatenate([lower, upper], axis=1).astype(jnp.bfloat16)
+
+
+def layer_kernel(n_dev, near_scale, far_scale, item_ref, spot_ref, leaves_ref, base_ref,
+                 near_ref, far_ref, below1, above1, below2, above2, below3, above3, points,
+                 targets, results, outbox, inbox, mine, sibling, line_recv, line_send,
+                 point_send, point_recv, sum_send, sum_recv, node_send, node_recv):
+    planes = n_dev // 8
+    depth_count = n_dev.bit_length() - 1
+    leaves_dev = leaves_ref.shape[0]
+    half = leaves_dev // 2
+    held = (leaves_ref, below1, above1, below2, above2, below3, above3)
+    me = lax.axis_index("leaf")
+    bits = [(me // 2**level) % 2 for level in range(depth_count)]
+    partners = [me + (1 - 2 * bits[level]) * 2**level for level in range(depth_count)]
+    plane = me // 8
+
+    def peer(apart):
+        found = me
+        for level in range(3):
+            found = found + (1 - 2 * bits[level]) * 2**level * (apart // 2**level % 2)
+        return found
+
+    def remote(source, target, send_sem, recv_sem, device):
+        return pltpu.make_async_remote_copy(
+            src_ref=source, dst_ref=target, send_sem=send_sem, recv_sem=recv_sem,
+            device_id=(device,), device_id_type=pl.DeviceIdType.MESH,
+        )
+
+    barrier = pltpu.get_barrier_semaphore()
+
+    def greet(device):
+        pl.semaphore_signal(
+            barrier, inc=1, device_id=(device,), device_id_type=pl.DeviceIdType.MESH
+        )
+
+    for device in [peer(apart) for apart in range(1, 8)] + partners[4:]:
+        greet(device)
+
+    @pl.when(plane < planes - 1)
+    def _():
+        greet(me + 8)
+
+    @pl.when(plane > 0)
+    def _():
+        greet(me - 8)
+
+    pl.semaphore_wait(
+        barrier,
+        7 + len(partners[4:]) + jnp.where(plane < planes - 1, 1, 0) + jnp.where(plane > 0, 1, 0),
+    )
+
+    def line_copy(step, above, part):
+        target = 2 * step - 1 + above
+        source = 0 if step == 1 else target - 2
+        piece = pl.ds(part * half, half)
+        return remote(
+            held[source].at[piece], held[target].at[piece], line_send.at[target - 1, part],
+            line_recv.at[target - 1, part], me - 8 if above else me + 8,
+        )
+
+    def sends(step, above):
+        if above:
+            return (plane > 0) & (plane + step - 1 < planes)
+        return (plane < planes - 1) & (plane - step + 1 >= 0)
+
+    def receives(step, above):
+        return plane + step < planes if above else plane - step >= 0
+
+    def line_step(step):
+        for part in range(2):
+            for above in range(2):
+                @pl.when(receives(step, above))
+                def _():
+                    line_copy(step, above, part).wait_recv()
+                if step + 1 < planes:
+                    @pl.when(sends(step + 1, above))
+                    def _():
+                        line_copy(step + 1, above, part).start()
+
+    def point_copy(apart):
+        return remote(
+            leaves_ref.at[:, pl.ds(0, D)], points.at[apart], point_send.at[apart],
+            point_recv.at[apart], peer(apart),
+        )
+
+    def sum_copy(apart):
+        return remote(
+            outbox.at[apart], inbox.at[apart], sum_send.at[apart], sum_recv.at[apart], peer(apart)
+        )
+
+    def node_copy(level):
+        return remote(
+            mine.at[level], sibling.at[level], node_send.at[level], node_recv.at[level],
+            partners[level],
+        )
+
+    def columns(leaf):
+        return pl.ds(pl.multiple_of(leaf * LEAF, LEAF), LEAF)
+
+    def self_leaf(leaf, carry):
+        target = target_side(leaves_ref[leaf, :D, :])
+        targets[leaf] = target
+        near_ref[:, columns(leaf)] = tile_term(
+            target, leaves_ref[leaf, :D, :], leaves_ref[leaf, D:, :]
+        ).T
+        far_ref[:, columns(leaf)] = jnp.zeros((RHS, LEAF), jnp.float32)
+        return carry
+
+    def far_levels(first, last):
+        def item(index, carry):
+            level = first + index // leaves_dev
+            leaf = index % leaves_dev
+            term = tile_term(targets[leaf], sibling[level, :D, :], sibling[level, D:, :])
+            far_ref[:, columns(leaf)] += term.T
+            return carry
+        lax.fori_loop(0, (last - first) * leaves_dev, item, 0)
+
+    def next_node(level):
+        node_copy(level).wait_recv()
+        if level + 1 < depth_count:
+            mine[level + 1] = merged(mine[level], sibling[level], bits[level])
+            node_copy(level + 1).start()
+
+    def prepare(apart, carry):
+        point_copy(apart).wait_recv()
+
+        def one_leaf(leaf, inner):
+            targets[apart * leaves_dev + leaf] = target_side(points[apart, leaf])
+            return inner
+        return lax.fori_loop(0, leaves_dev, one_leaf, carry)
+
+    def finish(apart):
+        def leaf_sum(leaf):
+            first = (apart * leaves_dev + leaf) * NEAR
+            total = results[spot_ref[first]]
+            for slot in range(1, NEAR):
+                total = total + results[spot_ref[first + slot]]
+            return total
+
+        @pl.when(apart == 0)
+        def _():
+            def own_leaf(leaf, carry):
+                near_ref[:, columns(leaf)] += leaf_sum(leaf)
+                return carry
+            lax.fori_loop(0, leaves_dev, own_leaf, 0)
+
+        @pl.when(apart > 0)
+        def _():
+            def peer_leaf(leaf, carry):
+                outbox[apart, :, columns(leaf)] = leaf_sum(leaf).astype(jnp.bfloat16)
+                return carry
+            lax.fori_loop(0, leaves_dev, peer_leaf, 0)
+            sum_copy(apart).start()
+
+    def near_group(group, is_last):
+        def readers(index, carry):
+            apart = 7 - index
+
+            def item(rank, inner):
+                spot = (group * 8 + apart) * PER_PAIR + rank
+                block = held[group][item_ref[1, spot]]
+                target = targets[apart * leaves_dev + item_ref[0, spot]]
+                results[spot] = tile_term(target, block[:D], block[D:]).T
+                return inner
+            lax.fori_loop(0, PER_PAIR, item, 0)
+            if is_last is not None:
+                @pl.when(is_last)
+                def _():
+                    finish(apart)
+            return carry
+        lax.fori_loop(0, 7 if group == 0 else 8, readers, 0)
+
+    def line_groups(step):
+        for above in range(2):
+            @pl.when(receives(step, above))
+            def _():
+                last = None
+                if step >= planes // 2:
+                    farther = plane < planes - 1 - plane
+                    reach = jnp.where(farther, planes - 1 - plane, plane)
+                    side = jnp.where(farther, 1, 0)
+                    last = (reach == step) & (side == above)
+                near_group(2 * step - 1 + above, last)
+
+    for part in range(2):
+        for above in range(2):
+            @pl.when(sends(1, above))
+            def _():
+                line_copy(1, above, part).start()
+    mine[0] = base_ref[...]
+    node_copy(0).start()
+    for apart in range(1, 8):
+        point_copy(apart).start()
+    results[7 * 8 * PER_PAIR] = jnp.zeros((RHS, LEAF), jnp.float32)
+    lax.fori_loop(0, leaves_dev, self_leaf, 0)
+    early = min(3, depth_count)
+    for level in range(early):
+        next_node(level)
+    far_levels(0, early)
+    line_step(1)
+    for level in range(early, depth_count):
+        next_node(level)
+    far_levels(early, depth_count)
+    lax.fori_loop(1, 8, prepare, 0)
+    near_group(0, None)
+    for step in range(2, planes):
+        line_step(step)
+        line_groups(step - 1)
+    line_groups(planes - 1)
+
+    for apart in range(1, 8):
+        sum_copy(apart).wait_recv()
+
+    def scale(leaf, carry):
+        total = near_ref[:, columns(leaf)]
+        for apart in range(1, 8):
+            total = total + inbox[apart, :, columns(leaf)].astype(jnp.float32)
+        near_ref[:, columns(leaf)] = total * near_scale
+        far_ref[:, columns(leaf)] = far_ref[:, columns(leaf)] * far_scale
+        return carry
+    lax.fori_loop(0, leaves_dev, scale, 0)
+
+    for level in range(depth_count):
+        node_copy(level).wait_send()
+    for apart in range(1, 8):
+        point_copy(apart).wait_send()
+        sum_copy(apart).wait_send()
+    for step in range(1, planes):
+        for part in range(2):
+            for above in range(2):
+                @pl.when(sends(step, above))
+                def _():
+                    line_copy(step, above, part).wait_send()
+
+
+def fused(leaf_blocks, base_node, near_leaf, near_count, n_dev, my_index):
+    leaves_dev = leaf_blocks.shape[0]
+    p_dev = leaves_dev * LEAF
+    slot_count = leaves_dev * NEAR
+    depth_count = n_dev.bit_length() - 1
+    planes = n_dev // 8
+    spots = 7 * 8 * PER_PAIR
+
+    readers = my_index ^ jnp.arange(8, dtype=jnp.int32)
+    leaf_ids = near_leaf.reshape(n_dev, slot_count)[readers]
+    counts = near_count.reshape(n_dev, leaves_dev)[readers]
+    slot = jnp.arange(slot_count, dtype=jnp.int32)
+    owner = leaf_ids // leaves_dev
+    live = slot % NEAR < jnp.repeat(counts, NEAR, axis=1)
+    live = live & (owner % 8 == my_index % 8)
+    apart = owner // 8 - my_index // 8
+    group = jnp.where(apart == 0, 0, 2 * jnp.abs(apart) - jnp.where(apart < 0, 1, 0))
+    earlier = (slot[None, :] < slot[:, None])[None] & live[:, None, :]
+    earlier = earlier & (group[:, None, :] == group[:, :, None])
+    rank = jnp.sum(earlier.astype(jnp.int32), axis=2)
+    reader = jnp.arange(8, dtype=jnp.int32)[:, None]
+    spot = jnp.where(live, (group * 8 + reader) * PER_PAIR + rank, spots).astype(jnp.int32)
+    fields = (slot[None, :] // NEAR) * leaves_dev + leaf_ids % leaves_dev
+    spot = spot.reshape(-1)
+    chosen = spot[None, :] == jnp.arange(spots, dtype=jnp.int32)[:, None]
+    packed = jnp.sum(jnp.where(chosen, fields.reshape(1, -1), 0), axis=1).astype(jnp.int32)
+    items = jnp.stack([packed // leaves_dev, packed % leaves_dev])
+
+    tiles = leaves_dev * (depth_count + 1) + planes * 8 * PER_PAIR
+    whole = pl.BlockSpec(memory_space=pltpu.VMEM)
+    scalars = pl.BlockSpec(memory_space=pltpu.SMEM)
+    dma = pltpu.SemaphoreType.DMA
+    block_buffer = pltpu.VMEM((leaves_dev, ROWS, LEAF), jnp.bfloat16)
+    return pl.pallas_call(
+        functools.partial(
+            layer_kernel, n_dev, 4.0 / math.sqrt(LEAF * (NEAR + 1)),
+            4.0 / math.sqrt(p_dev * n_dev),
+        ),
+        in_specs=[scalars, scalars, whole, whole],
+        out_specs=[whole, whole],
+        out_shape=[jax.ShapeDtypeStruct((RHS, p_dev), jnp.float32)] * 2,
+        scratch_shapes=[
+            *[block_buffer] * 6,
+            pltpu.VMEM((8, leaves_dev, D, LEAF), jnp.bfloat16),
+            pltpu.VMEM((8 * leaves_dev, LEAF, DEPTH), jnp.bfloat16),
+            pltpu.VMEM((spots + 1, RHS, LEAF), jnp.float32),
+            pltpu.VMEM((8, RHS, p_dev), jnp.bfloat16),
+            pltpu.VMEM((8, RHS, p_dev), jnp.bfloat16),
+            pltpu.VMEM((depth_count, ROWS, SKEL), jnp.bfloat16),
+            pltpu.VMEM((depth_count, ROWS, SKEL), jnp.bfloat16),
+            dma((6, 2)),
+            dma((6, 2)),
+            dma((8,)),
+            dma((8,)),
+            dma((8,)),
+            dma((8,)),
+            dma((depth_count,)),
+            dma((depth_count,)),
+        ],
+        compiler_params=pltpu.CompilerParams(
+            collective_id=0, has_side_effects=True, vmem_limit_bytes=60 * 2**20
+        ),
+        cost_estimate=pl.CostEstimate(
+            flops=tiles * 2 * LEAF * LEAF * (DEPTH + 256),
+            bytes_accessed=4 * 2**20,
+            transcendentals=tiles * LEAF * LEAF,
+        ),
+        name="exchange_and_tiles",
+    )(items, spot, leaf_blocks, base_node)
+
+
 def fold_child(nodes):
     half = nodes.shape[-1] // 2
     folded = nodes[..., D:, :half].astype(jnp.float32) + nodes[..., D:, half:].astype(jnp.float32)
@@ -136,6 +454,9 @@
     )
     base_node = jnp.concatenate([points[:, skel_index], base_weights.astype(jnp.bfloat16)], axis=0)
     stacked = jnp.concatenate([points, weights], axis=0)
+    if n_dev == 32 and PER_PAIR * (n_dev - 1) >= leaves_dev * NEAR:
+        leaf_blocks = stacked.reshape(ROWS, leaves_dev, LEAF).transpose(1, 0, 2)
+        return fused(leaf_blocks, base_node, near_leaf, near_count, n_dev, my_index)
     base_node, stacked = lax.optimization_barrier((base_node, stacked))
     nodes = lax.all_gather(base_node, "leaf")
     blocks = lax.all_gather(stacked, "leaf")

time: 286 us -> 209 us (0.73)
  waiting for transfers between devices: 194 us -> 0 us
  Pallas kernels: 65.7 us -> 194 us
  between operations: 14.4 us -> 0.83 us
    all_gather x2 -> x0, waiting for transfers between devices: 193 us -> none  [the longest x1 133 us: per_device(): blocks = lax.all_gather(stacked, 'leaf')]
    pallas_call x2 -> x1, Pallas kernels: 65.7 us -> 194 us  [fused(): pl.pallas_call(functools.partial(layer_kernel, n_dev, 4.0 / math.sqrt(LEA...]
  transfers between devices with their start and end apart: 2 -> 0, of which waited for: 2 -> 0; matrix products, arithmetic and copies ran while one was open for 2% -> 0% of each run, Pallas kernels for 7% -> 0%
where the time goes in v3:
time: 209 us
  Pallas kernels  194 us (93%)
  local copies, waits for them, and re-layouts  9.29 us (4%)
  other arithmetic  2.92 us (1%)
    pallas_call x1, Pallas kernels, fused(): pl.pallas_call(functools.partial(layer_kernel, n_dev, 4.0 / math.sqrt(LEA...  194 us
    unnamed x16, local copies, waits for them, and re-layouts  4.29 us

profile of v3, /device:TPU:0, one launch (start us, length us, event | category | flops | bytes accessed | tf_op | source)
XLA Modules:
  0.0 209.0 jit_solution(2348907620291973873)
XLA Ops:
  0.6 0.0 copy-start
  0.7 0.9 copy.15
  1.6 0.1 reshape.389
  1.7 0.6 gather_fusion.1
  2.2 0.8 reshape.387
  3.0 0.6 gather_fusion
  3.5 0.1 broadcast_in_dim.22
  3.6 0.1 reshape.390
  3.8 0.4 convert_reduce_fusion
  4.2 0.1 reduce_sum.23
  4.2 0.1 gather.13
  4.3 0.1 reshape.388
  4.4 0.1 lt.109
  4.5 0.1 add.164
  4.6 0.1 add.159
  4.7 0.0 copy-start.3
  4.7 0.2 select_reduce_fusion
  4.9 0.6 pad_add_fusion.item_ref
  5.5 0.0 copy-done
  5.5 1.0 pad_maximum_fusion
  6.5 1.0 copy.21
  7.5 0.0 copy-done.3
  7.5 0.5 copy.17
  8.0 0.2 copy-done.4
  8.2 1.3 gather_fusion.2
  9.5 0.1 copy.18
  9.6 0.0 copy-done.2
  9.6 1.5 fusion.3
  11.2 0.7 pad_maximum_fusion.1.base_ref
  11.8 194.4 %exchange_and_tiles.1 = (f32[32,4096]{1,0:T(8,128)}, f32[32,4096]{1,0:T(8,128)}) custom-call(s32[2,224]{1,0:T(2,128)} %pad_add_fusion.item_ref, s32[768]{0:T(1024)} %copy-done.3, bf16[8,96,512]{2,1,0:T(8,128)(2,1)} %bitcast.15, bf16[96,512]{1,0:T(8,128)(2,1)} %pad_maximum_fusion.1.base_ref), custom_call_target="tpu_custom_call" | custom-call | flops 47244640256 | bytes 4194304 | tf_op jit(solution)/shard_map/exchange_and_tiles/pallas_call | solution.py:390
  206.3 1.9 copy.24
  208.2 0.8 copy.25
  (21 shorter events, 0.2 us)
Async XLA Ops:
  0.6 4.9 %copy-start = (bf16[64,4096]{1,0:T(8,128)(2,1)S(1)}, bf16[64,4096]{1,0:T(8,128)(2,1)}, u32[]{:S(2)}) copy-start(bf16[64,4096]{1,0:T(8,128)(2,1)} %param.6) | copy-start | bytes 1572868
  4.7 2.8 %copy-start.3 = (s32[768]{0:T(1024)}, s32[768]{0:T(1024)S(1)}, u32[]{:S(2)}) copy-start(s32[768]{0:T(1024)S(1)} %get-tuple-element.4.spot_ref) | copy-start | bytes 9220
  7.5 0.7 copy-start.4
  7.5 2.1 %copy-start.2 = (bf16[32,4096]{1,0:T(8,128)(2,1)S(1)}, bf16[32,4096]{1,0:T(8,128)(2,1)}, u32[]{:S(2)}) copy-start(bf16[32,4096]{1,0:T(8,128)(2,1)} %param.7) | copy-start | bytes 786436
  7.5 2.2 %copy-start.5 = (s32[4096]{0:T(1024)S(1)}, s32[4096]{0:T(1024)}, u32[]{:S(2)}) copy-start(s32[4096]{0:T(1024)} %param.9) | copy-start | bytes 49156
  206.3 1.9 copy-start.1

commit v4 on v3

--- a/solution.py
+++ b/solution.py
@@ -17,6 +17,7 @@
 DEPTH = 256
 SCALE2 = 1.0 / (D * math.log(2.0))
 SLOTS = 4
+TAIL = 16
 PER_PAIR = 4
 
 
@@ -41,16 +42,23 @@
     return tail
 
 
+def spare_rows(points):
+    return jnp.zeros((DEPTH - 3 * D - TAIL, points.shape[1]), jnp.bfloat16)
+
+
 def target_side(points):
     points32 = points.astype(jnp.float32)
     parts = three_parts(points32 * (2.0 * SCALE2))
-    tail = tail_rows(neg_norm_parts(points32), 3, 0, DEPTH - 3 * D)
-    return jnp.concatenate([*parts, tail], axis=0).T.astype(jnp.bfloat16)
+    tail = tail_rows(neg_norm_parts(points32), 3, 0, TAIL)
+    rows = [part.astype(jnp.bfloat16) for part in (*parts, tail)]
+    return jnp.concatenate(rows + [spare_rows(points)], axis=0).T
 
 
 def source_side(points):
-    tail = tail_rows(neg_norm_parts(points.astype(jnp.float32)), 0, 3, DEPTH - 3 * D)
-    return jnp.concatenate([points, points, points, tail.astype(jnp.bfloat16)], axis=0)
+    tail = tail_rows(neg_norm_parts(points.astype(jnp.float32)), 0, 3, TAIL)
+    return jnp.concatenate(
+        [points, points, points, tail.astype(jnp.bfloat16), spare_rows(points)], axis=0
+    )
 
 
 def tile_term(target, points, weights):
@@ -198,11 +206,31 @@
                     def _():
                         line_copy(step + 1, above, part).start()
 
-    def point_copy(apart):
+    def point_copy(apart, part=None):
+        if apart in (1, 2, 4):
+            source, over = leaves_ref.at[:, pl.ds(0, D)], apart
+        elif apart == 6:
+            source, over = points.at[2 + 2 * part], 4 - 2 * part
+        else:
+            source, over = points.at[apart - 1], 1
+        target = points.at[apart]
+        if part is not None:
+            source, target = source.at[pl.ds(part * half, half)], target.at[pl.ds(part * half, half)]
+        slot = 0 if part is None else part
         return remote(
-            leaves_ref.at[:, pl.ds(0, D)], points.at[apart], point_send.at[apart],
-            point_recv.at[apart], peer(apart),
-        )
+            source, target, point_send.at[apart, slot], point_recv.at[apart, slot], peer(over)
+        )
+
+    def relay_sides():
+        for apart, part in ((2, 0), (4, 1)):
+            point_copy(apart).wait_recv()
+            point_copy(6, part).start()
+            point_copy(apart + 1).start()
+
+    def relay_across():
+        for part in range(2):
+            point_copy(6, part).wait_recv()
+        point_copy(7).start()
 
     def sum_copy(apart):
         return remote(
@@ -228,13 +256,14 @@
         return carry
 
     def far_levels(first, last):
-        def item(index, carry):
-            level = first + index // leaves_dev
-            leaf = index % leaves_dev
-            term = tile_term(targets[leaf], sibling[level, :D, :], sibling[level, D:, :])
+        def item(leaf, carry):
+            target = targets[leaf]
+            term = jnp.zeros((LEAF, RHS), jnp.float32)
+            for level in range(first, last):
+                term = term + tile_term(target, sibling[level, :D, :], sibling[level, D:, :])
             far_ref[:, columns(leaf)] += term.T
             return carry
-        lax.fori_loop(0, (last - first) * leaves_dev, item, 0)
+        lax.fori_loop(0, leaves_dev, item, 0)
 
     def next_node(level):
         node_copy(level).wait_recv()
@@ -243,8 +272,6 @@
             node_copy(level + 1).start()
 
     def prepare(apart, carry):
-        point_copy(apart).wait_recv()
-
         def one_leaf(leaf, inner):
             targets[apart * leaves_dev + leaf] = target_side(points[apart, leaf])
             return inner
@@ -277,13 +304,15 @@
         def readers(index, carry):
             apart = 7 - index
 
-            def item(rank, inner):
-                spot = (group * 8 + apart) * PER_PAIR + rank
-                block = held[group][item_ref[1, spot]]
-                target = targets[apart * leaves_dev + item_ref[0, spot]]
-                results[spot] = tile_term(target, block[:D], block[D:]).T
-                return inner
-            lax.fori_loop(0, PER_PAIR, item, 0)
+            first = (group * 8 + apart) * PER_PAIR
+            total = jnp.zeros((LEAF, PER_PAIR * RHS), jnp.float32)
+            for rank in range(PER_PAIR):
+                block = held[group][item_ref[1, first + rank]]
+                target = targets[apart * leaves_dev + item_ref[0, first + rank]]
+                weights = [jnp.zeros((RHS, LEAF), jnp.bfloat16)] * PER_PAIR
+                weights[rank] = block[D:]
+                total = total + tile_term(target, block[:D], jnp.concatenate(weights, axis=0))
+            results[pl.ds(first, PER_PAIR)] = total.T.reshape(PER_PAIR, RHS, LEAF)
             if is_last is not None:
                 @pl.when(is_last)
                 def _():
@@ -310,22 +339,28 @@
                 line_copy(1, above, part).start()
     mine[0] = base_ref[...]
     node_copy(0).start()
-    for apart in range(1, 8):
+    for apart in (1, 2, 4):
         point_copy(apart).start()
     results[7 * 8 * PER_PAIR] = jnp.zeros((RHS, LEAF), jnp.float32)
     lax.fori_loop(0, leaves_dev, self_leaf, 0)
+    relay_sides()
     early = min(3, depth_count)
     for level in range(early):
         next_node(level)
     far_levels(0, early)
     line_step(1)
+    relay_across()
     for level in range(early, depth_count):
         next_node(level)
     far_levels(early, depth_count)
+    for apart in (1, 3, 5, 7):
+        point_copy(apart).wait_recv()
+    line_step(2)
     lax.fori_loop(1, 8, prepare, 0)
     near_group(0, None)
     for step in range(2, planes):
-        line_step(step)
+        if step > 2:
+            line_step(step)
         line_groups(step - 1)
     line_groups(planes - 1)
 
@@ -344,7 +379,11 @@
     for level in range(depth_count):
         node_copy(level).wait_send()
     for apart in range(1, 8):
-        point_copy(apart).wait_send()
+        if apart == 6:
+            point_copy(6, 0).wait_send()
+            point_copy(6, 1).wait_send()
+        else:
+            point_copy(apart).wait_send()
         sum_copy(apart).wait_send()
     for step in range(1, planes):
         for part in range(2):
@@ -406,8 +445,8 @@
             pltpu.VMEM((depth_count, ROWS, SKEL), jnp.bfloat16),
             dma((6, 2)),
             dma((6, 2)),
-            dma((8,)),
-            dma((8,)),
+            dma((8, 2)),
+            dma((8, 2)),
             dma((8,)),
             dma((8,)),
             dma((depth_count,)),

time: 209 us -> 164 us (0.78)
  Pallas kernels: 194 us -> 149 us
    pallas_call x1, Pallas kernels: 194 us -> 149 us  [fused(): pl.pallas_call(functools.partial(layer_kernel, n_dev, 4.0 / math.sqrt(LEA...]
where the time goes in v4:
time: 164 us; the launch traced here: 163 us
  Pallas kernels  149 us (91%)
  local copies, waits for them, and re-layouts  9.29 us (6%)
  other arithmetic  2.92 us (2%)
    pallas_call x1, Pallas kernels, fused(): pl.pallas_call(functools.partial(layer_kernel, n_dev, 4.0 / math.sqrt(LEA...  149 us
    unnamed x16, local copies, waits for them, and re-layouts  4.29 us

profile of v4, /device:TPU:0, one launch (start us, length us, event | category | flops | bytes accessed | tf_op | source)
XLA Modules:
  0.0 163.2 jit_solution(5987968587715865687)
XLA Ops:
  0.6 0.0 copy-start
  0.7 0.9 copy.15
  1.6 0.1 reshape.389
  1.7 0.6 gather_fusion.1
  2.2 0.8 reshape.387
  3.0 0.6 gather_fusion
  3.5 0.1 broadcast_in_dim.22
  3.6 0.1 reshape.390
  3.8 0.4 convert_reduce_fusion
  4.2 0.1 reduce_sum.23
  4.2 0.1 gather.13
  4.3 0.1 reshape.388
  4.4 0.1 lt.109
  4.5 0.1 add.164
  4.6 0.1 add.159
  4.7 0.0 copy-start.3
  4.7 0.2 select_reduce_fusion
  4.9 0.6 pad_add_fusion.item_ref
  5.5 0.0 copy-done
  5.5 1.0 pad_maximum_fusion
  6.5 1.0 copy.21
  7.5 0.0 copy-done.3
  7.5 0.5 copy.17
  8.0 0.2 copy-done.4
  8.2 1.3 gather_fusion.2
  9.5 0.1 copy.18
  9.6 0.0 copy-done.2
  9.6 1.5 fusion.3
  11.2 0.7 pad_maximum_fusion.1.base_ref
  11.8 148.7 %exchange_and_tiles.1 = (f32[32,4096]{1,0:T(8,128)}, f32[32,4096]{1,0:T(8,128)}) custom-call(s32[2,224]{1,0:T(2,128)} %pad_add_fusion.item_ref, s32[768]{0:T(1024)} %copy-done.3, bf16[8,96,512]{2,1,0:T(8,128)(2,1)} %bitcast.15, bf16[96,512]{1,0:T(8,128)(2,1)} %pad_maximum_fusion.1.base_ref), custom_call_target="tpu_custom_call" | custom-call | flops 47244640256 | bytes 4194304 | tf_op jit(solution)/shard_map/exchange_and_tiles/pallas_call | solution.py:429
  160.5 1.9 %copy.24 = f32[32,4096]{1,0:T(8,128)} copy(f32[32,4096]{1,0:T(8,128)} %get-tuple-element.8) | data formatting | bytes 1048576
  162.5 0.8 copy.25
  (21 shorter events, 0.2 us)
Async XLA Ops:
  0.6 4.9 %copy-start = (bf16[64,4096]{1,0:T(8,128)(2,1)S(1)}, bf16[64,4096]{1,0:T(8,128)(2,1)}, u32[]{:S(2)}) copy-start(bf16[64,4096]{1,0:T(8,128)(2,1)} %param.6) | copy-start | bytes 1572868
  4.7 2.8 %copy-start.3 = (s32[768]{0:T(1024)}, s32[768]{0:T(1024)S(1)}, u32[]{:S(2)}) copy-start(s32[768]{0:T(1024)S(1)} %get-tuple-element.4.spot_ref) | copy-start | bytes 9220
  7.5 0.7 copy-start.4
  7.5 2.1 %copy-start.2 = (bf16[32,4096]{1,0:T(8,128)(2,1)S(1)}, bf16[32,4096]{1,0:T(8,128)(2,1)}, u32[]{:S(2)}) copy-start(bf16[32,4096]{1,0:T(8,128)(2,1)} %param.7) | copy-start | bytes 786436
  7.5 2.2 %copy-start.5 = (s32[4096]{0:T(1024)S(1)}, s32[4096]{0:T(1024)}, u32[]{:S(2)}) copy-start(s32[4096]{0:T(1024)} %param.9) | copy-start | bytes 49156
  160.5 1.9 %copy-start.1 = (f32[32,4096]{1,0:T(8,128)S(1)}, f32[32,4096]{1,0:T(8,128)}, u32[]{:S(2)}) copy-start(f32[32,4096]{1,0:T(8,128)} %get-tuple-element.9) | copy-start | bytes 1572868

commit v5 on v4

--- a/solution.py
+++ b/solution.py
@@ -18,6 +18,7 @@
 SCALE2 = 1.0 / (D * math.log(2.0))
 SLOTS = 4
 TAIL = 16
+PARTS = 4
 PER_PAIR = 4
 
 
@@ -136,7 +137,7 @@
     planes = n_dev // 8
     depth_count = n_dev.bit_length() - 1
     leaves_dev = leaves_ref.shape[0]
-    half = leaves_dev // 2
+    half, share = leaves_dev // 2, leaves_dev // PARTS
     held = (leaves_ref, below1, above1, below2, above2, below3, above3)
     me = lax.axis_index("leaf")
     bits = [(me // 2**level) % 2 for level in range(depth_count)]
@@ -181,7 +182,7 @@
     def line_copy(step, above, part):
         target = 2 * step - 1 + above
         source = 0 if step == 1 else target - 2
-        piece = pl.ds(part * half, half)
+        piece = pl.ds(part * share, share)
         return remote(
             held[source].at[piece], held[target].at[piece], line_send.at[target - 1, part],
             line_recv.at[target - 1, part], me - 8 if above else me + 8,
@@ -196,7 +197,7 @@
         return plane + step < planes if above else plane - step >= 0
 
     def line_step(step):
-        for part in range(2):
+        for part in range(PARTS):
             for above in range(2):
                 @pl.when(receives(step, above))
                 def _():
@@ -332,7 +333,7 @@
                     last = (reach == step) & (side == above)
                 near_group(2 * step - 1 + above, last)
 
-    for part in range(2):
+    for part in range(PARTS):
         for above in range(2):
             @pl.when(sends(1, above))
             def _():
@@ -350,19 +351,20 @@
     far_levels(0, early)
     line_step(1)
     relay_across()
-    for level in range(early, depth_count):
-        next_node(level)
-    far_levels(early, depth_count)
     for apart in (1, 3, 5, 7):
         point_copy(apart).wait_recv()
+    lax.fori_loop(1, 8, prepare, 0)
     line_step(2)
-    lax.fori_loop(1, 8, prepare, 0)
+    for level in range(early, depth_count - 1):
+        next_node(level)
     near_group(0, None)
-    for step in range(2, planes):
-        if step > 2:
-            line_step(step)
-        line_groups(step - 1)
-    line_groups(planes - 1)
+    line_groups(1)
+    next_node(depth_count - 1)
+    far_levels(early, depth_count)
+    line_groups(2)
+    for step in range(3, planes):
+        line_step(step)
+        line_groups(step)
 
     for apart in range(1, 8):
         sum_copy(apart).wait_recv()
@@ -386,7 +388,7 @@
             point_copy(apart).wait_send()
         sum_copy(apart).wait_send()
     for step in range(1, planes):
-        for part in range(2):
+        for part in range(PARTS):
             for above in range(2):
                 @pl.when(sends(step, above))
                 def _():
@@ -443,8 +445,8 @@
             pltpu.VMEM((8, RHS, p_dev), jnp.bfloat16),
             pltpu.VMEM((depth_count, ROWS, SKEL), jnp.bfloat16),
             pltpu.VMEM((depth_count, ROWS, SKEL), jnp.bfloat16),
-            dma((6, 2)),
-            dma((6, 2)),
+            dma((6, PARTS)),
+            dma((6, PARTS)),
             dma((8, 2)),
             dma((8, 2)),
             dma((8,)),

time: 164 us -> 152 us (0.927)
  Pallas kernels: 149 us -> 137 us
    pallas_call x1, Pallas kernels: 149 us -> 137 us  [fused(): pl.pallas_call(functools.partial(layer_kernel, n_dev, 4.0 / math.sqrt(LEA...]
where the time goes in v5:
time: 152 us; the launch traced here: 151 us
  Pallas kernels  137 us (90%)
  local copies, waits for them, and re-layouts  9.29 us (6%)
  other arithmetic  2.92 us (2%)
  matrix products  1.53 us (1%)
    pallas_call x1, Pallas kernels, fused(): pl.pallas_call(functools.partial(layer_kernel, n_dev, 4.0 / math.sqrt(LEA...  137 us
    unnamed x16, local copies, waits for them, and re-layouts  4.29 us

profile of v5, /device:TPU:0, one launch (start us, length us, event | category | flops | bytes accessed | tf_op | source)
XLA Modules:
  0.0 151.5 jit_solution(4079626182548416348)
XLA Ops:
  0.6 0.0 copy-start
  0.7 0.9 copy.15
  1.6 0.1 reshape.389
  1.7 0.6 gather_fusion.1
  2.2 0.8 reshape.387
  3.0 0.6 gather_fusion
  3.5 0.1 broadcast_in_dim.22
  3.6 0.1 reshape.390
  3.8 0.4 convert_reduce_fusion
  4.2 0.1 reduce_sum.23
  4.2 0.1 gather.13
  4.3 0.1 reshape.388
  4.4 0.1 lt.109
  4.5 0.1 add.164
  4.6 0.1 add.159
  4.7 0.0 copy-start.3
  4.7 0.2 select_reduce_fusion
  4.9 0.6 pad_add_fusion.item_ref
  5.5 0.0 copy-done
  5.5 1.0 pad_maximum_fusion
  6.5 1.0 copy.21
  7.5 0.5 copy.17
  8.0 0.2 copy-done.4
  8.2 1.3 gather_fusion.2
  9.5 0.1 copy.18
  9.6 0.0 copy-done.2
  9.6 0.0 copy-done.5
  9.6 1.5 %fusion.3 = bf16[32,512]{1,0:T(8,128)(2,1)S(1)} fusion(bf16[32,4096]{1,0:T(8,128)(2,1)S(1)} %copy-done.2, s32[4096]{0:T(1024)S(1)} %copy-done.5), kind=kOutput, calls=%fused_computation.7 | convolution fusion | flops 136331264 | bytes 311296 | tf_op jit(solution)/shard_map/dot_general | solution.py:493
  11.2 0.7 pad_maximum_fusion.1.base_ref
  11.8 136.9 %exchange_and_tiles.1 = (f32[32,4096]{1,0:T(8,128)}, f32[32,4096]{1,0:T(8,128)}) custom-call(s32[2,224]{1,0:T(2,128)} %pad_add_fusion.item_ref, s32[768]{0:T(1024)} %copy-done.3, bf16[8,96,512]{2,1,0:T(8,128)(2,1)} %bitcast.15, bf16[96,512]{1,0:T(8,128)(2,1)} %pad_maximum_fusion.1.base_ref), custom_call_target="tpu_custom_call" | custom-call | flops 47244640256 | bytes 4194304 | tf_op jit(solution)/shard_map/exchange_and_tiles/pallas_call | solution.py:431
  148.8 1.9 %copy.24 = f32[32,4096]{1,0:T(8,128)} copy(f32[32,4096]{1,0:T(8,128)} %get-tuple-element.8) | data formatting | bytes 1048576
  150.7 0.8 copy.25
  (21 shorter events, 0.2 us)
Async XLA Ops:
  0.6 4.9 %copy-start = (bf16[64,4096]{1,0:T(8,128)(2,1)S(1)}, bf16[64,4096]{1,0:T(8,128)(2,1)}, u32[]{:S(2)}) copy-start(bf16[64,4096]{1,0:T(8,128)(2,1)} %param.6) | copy-start | bytes 1572868
  4.7 2.8 %copy-start.3 = (s32[768]{0:T(1024)}, s32[768]{0:T(1024)S(1)}, u32[]{:S(2)}) copy-start(s32[768]{0:T(1024)S(1)} %get-tuple-element.4.spot_ref) | copy-start | bytes 9220
  7.5 0.7 copy-start.4
  7.5 2.1 %copy-start.2 = (bf16[32,4096]{1,0:T(8,128)(2,1)S(1)}, bf16[32,4096]{1,0:T(8,128)(2,1)}, u32[]{:S(2)}) copy-start(bf16[32,4096]{1,0:T(8,128)(2,1)} %param.7) | copy-start | bytes 786436
  7.5 2.2 %copy-start.5 = (s32[4096]{0:T(1024)S(1)}, s32[4096]{0:T(1024)}, u32[]{:S(2)}) copy-start(s32[4096]{0:T(1024)} %param.9) | copy-start | bytes 49156
  148.8 1.9 %copy-start.1 = (f32[32,4096]{1,0:T(8,128)S(1)}, f32[32,4096]{1,0:T(8,128)}, u32[]{:S(2)}) copy-start(f32[32,4096]{1,0:T(8,128)} %get-tuple-element.9) | copy-start | bytes 1572868
